TPU v7x, 32 devices: a whole 2x2x4 slice. The times are simulated.
32 devices in a mesh: dp: 4 (over y, x), expert: 4 (over z), tensor: 2 (over core).
Axes of the slice: x: 2, y: 2, z: 4, core: 2. Of those that a mesh axis runs over, the one named last changes fastest.
Arguments:
- tokens: bfloat16 [2048, 2048], P(('dp', 'expert'), 'tensor'), may hold values from -6 to 6
- expert_ids: int32 [2048, 8], P(('dp', 'expert')), may hold values from 0 to 127, as said below
- route_weight: float32 [2048, 8], P(('dp', 'expert')), may hold values from 0.2 to 1
- gate_weight: bfloat16 [4, 2048, 768], P('expert', None, 'tensor'), may hold values from -0.125 to 0.125
- up_weight: bfloat16 [4, 2048, 768], P('expert', None, 'tensor'), may hold values from -0.125 to 0.125
- down_weight: bfloat16 [4, 768, 2048], P('expert', 'tensor'), may hold values from -0.21875 to 0.21875
- cotangent: bfloat16 [2048, 2048], P(('dp', 'expert'), 'tensor'), may hold values from -6 to 6
Outputs:
- mixed: bfloat16 [2048, 2048], P(('dp', 'expert'), 'tensor')
- token_grad: bfloat16 [2048, 2048], P(('dp', 'expert'), 'tensor')
- down_grad: bfloat16 [4, 768, 2048], P('expert', 'tensor', 'dp')
Inputs may be any that keep to these rules, and one draw needn't show every extreme that they name: `expert_ids`: among the rows of one device, at most 12 pairs choose the same expert; in every replica some expert below 4 is chosen by exactly 12 pairs on each of the replica's 4 devices; a token's choices are distinct.
All inputs are finite; a program needn't handle non-finite values.
Results may differ from a plain program's by a relative error of at most 0.017.
Values may be sent and summed in bfloat16 or wider, within the bound.
A program may use at most 64 MiB of HBM per device.

v0:
```python
import jax
import jax.numpy as jnp
from jax import lax
from jax.sharding import PartitionSpec as P

EXPERTS = 128


def tensor_rows(rows):
    return lax.all_gather(rows, "tensor", axis=2, tiled=True)


def tensor_total(partial_value):
    return lax.psum_scatter(
        partial_value.astype(jnp.bfloat16), "tensor", scatter_dimension=2, tiled=True
    )


def return_rows(rows):
    return lax.all_to_all(rows, "expert", split_axis=0, concat_axis=0, tiled=True)


def rounded(values):
    narrow = lax.optimization_barrier(tuple((v.astype(jnp.bfloat16) for v in values)))
    return tuple((v.astype(jnp.float32) for v in narrow))


def per_device(tokens, expert_ids, route_weight, gate_weight, up_weight, down_weight, cotangent):
    owners = lax.axis_size("expert")
    tok_rows, choose = expert_ids.shape
    capacity = 3 * tok_rows * choose // (2 * EXPERTS)
    npairs = tok_rows * choose
    feature_width = tokens.shape[1]
    slot_count = owners * capacity
    flat_ids = expert_ids.reshape(npairs)
    inside = flat_ids < owners
    onehot = (flat_ids[:, None] == jnp.arange(owners, dtype=jnp.int32)[None, :]).astype(jnp.int32)
    before = jnp.cumsum(onehot, axis=0) - onehot
    slot_rank = jnp.sum(before * onehot, axis=1)
    target = jnp.where(inside, flat_ids * capacity + slot_rank, slot_count)
    holder = (
        jnp.full((slot_count + 1,), npairs, jnp.int32)
        .at[target]
        .set(jnp.arange(npairs, dtype=jnp.int32))[:slot_count]
    )
    source_row = jnp.where(holder < npairs, holder // choose, tok_rows)
    tok_padded = jnp.concatenate([tokens, jnp.zeros((1, feature_width), jnp.bfloat16)], axis=0)
    send_rows = tok_padded[source_row].reshape(owners, capacity, feature_width)
    scaled = (
        jnp.repeat(cotangent.astype(jnp.float32), choose, axis=0) * route_weight.reshape(npairs, 1)
    ).astype(jnp.bfloat16)
    scaled_padded = jnp.concatenate([scaled, jnp.zeros((1, feature_width), jnp.bfloat16)], axis=0)
    grad_send = scaled_padded[holder].reshape(owners, capacity, feature_width)
    select = (jnp.arange(slot_count, dtype=jnp.int32)[:, None] == target[None, :]).astype(
        jnp.float32
    )
    select = select.reshape(slot_count, tok_rows, choose)
    combine = jnp.einsum("stk,tk->ts", select, route_weight, precision=lax.Precision.HIGHEST)
    collect = jnp.sum(select, axis=2).T
    w_gate = gate_weight[0]
    w_up = up_weight[0]
    w_down = down_weight[0]
    full_rows = tensor_rows(
        lax.all_to_all(send_rows, "expert", split_axis=0, concat_axis=0, tiled=True)
    )
    gate_pre = jnp.einsum("ncd,df->ncf", full_rows, w_gate, preferred_element_type=jnp.float32)
    up_pre = jnp.einsum("ncd,df->ncf", full_rows, w_up, preferred_element_type=jnp.float32)
    hidden = (gate_pre * jax.nn.sigmoid(gate_pre) * up_pre).astype(jnp.bfloat16)
    partial_value = jnp.einsum("ncf,fd->ncd", hidden, w_down, preferred_element_type=jnp.float32)
    returned, gate_pre, up_pre = (return_rows(tensor_total(partial_value)), gate_pre, up_pre)
    returned, gate_pre, up_pre = (returned, gate_pre, up_pre)
    grad_recv = lax.all_to_all(grad_send, "expert", split_axis=0, concat_axis=0, tiled=True)
    grad_full = tensor_rows(grad_recv)
    mixed = jnp.dot(
        combine,
        returned.reshape(slot_count, feature_width).astype(jnp.float32),
        precision=lax.Precision.HIGHEST,
    ).astype(jnp.bfloat16)
    hidden_grad = jnp.einsum("ncd,fd->ncf", grad_full, w_down, preferred_element_type=jnp.float32)
    sigmoid_gate = jax.nn.sigmoid(gate_pre)
    silu_gate = gate_pre * sigmoid_gate
    hidden = (silu_gate * up_pre).astype(jnp.bfloat16)
    gate_term = (
        hidden_grad * up_pre * sigmoid_gate * (1.0 + gate_pre * (1.0 - sigmoid_gate))
    ).astype(jnp.bfloat16)
    up_term = (hidden_grad * silu_gate).astype(jnp.bfloat16)
    full_d = grad_full.shape[2]
    hidden_width = hidden.shape[2]
    g_flat = grad_full.reshape(slot_count, full_d)
    h_flat = hidden.reshape(slot_count, hidden_width)
    own_down = jnp.einsum("rf,rd->fd", h_flat, g_flat, preferred_element_type=jnp.float32)
    down_round = rounded((own_down,))[0]
    sum_down = lax.psum_scatter(
        down_round.astype(jnp.bfloat16), "dp", scatter_dimension=1, tiled=True
    )
    part_grad = jnp.einsum("ncf,df->ncd", gate_term, w_gate, preferred_element_type=jnp.float32)
    part_grad = part_grad + jnp.einsum(
        "ncf,df->ncd", up_term, w_up, preferred_element_type=jnp.float32
    )
    grad_back = return_rows(tensor_total(part_grad))
    token_grad = jnp.dot(
        collect,
        grad_back.reshape(slot_count, feature_width).astype(jnp.float32),
        precision=lax.Precision.HIGHEST,
    ).astype(jnp.bfloat16)
    down_grad = sum_down[None]
    return (mixed, token_grad, down_grad)


def solution(mesh):
    placed = (
        P(("dp", "expert"), "tensor"),
        P(("dp", "expert"), None),
        P(("dp", "expert"), None),
        P("expert", None, "tensor"),
        P("expert", None, "tensor"),
        P("expert", "tensor", None),
        P(("dp", "expert"), "tensor"),
    )
    return jax.shard_map(
        per_device,
        mesh=mesh,
        in_specs=placed,
        out_specs=(
            P(("dp", "expert"), "tensor"),
            P(("dp", "expert"), "tensor"),
            P("expert", "tensor", "dp"),
        ),
        check_vma=False,
    )
```

profile of v0, /device:TPU:0, one launch (start us, length us, event | category | flops | bytes accessed | tf_op | source)
XLA Modules:
  0.0 107.8 jit_solution(3751155692019617933)
XLA Ops:
  7.2 0.0 copy-start
  7.2 0.0 copy-start.4
  7.2 0.9 copy.16
  8.1 0.1 eq.45
  8.2 0.1 eq.41
  8.3 1.1 %reduce-window.6 = s32[4,8,128]{2,1,0:T(8,128)S(1)} reduce-window(s32[4,8,128]{2,1,0:T(8,128)S(1)} %fusion.19, s32[]{:T(128)} %constant.18.clone.1), window={size=1x1x128 pad=0_0x0_0x127_0}, to_apply=%region_0.0 | reduce-window | flops 520192 | bytes 32772 | tf_op jit(solution)/shard_map/reduce-window
  9.5 0.2 slice_reduce_fusion
  9.7 0.2 reduce-window.9
  9.9 0.1 add_bitcast_fusion
  10.0 0.1 reduce_sum.23
  10.0 0.0 copy-start.6
  10.1 0.6 add_select_fusion
  10.7 0.1 lt.45
  10.8 0.1 mul.59
  10.9 4.3 %scatter_custom_fusion = s32[49]{0:T(128)S(1)} fusion(s32[1024]{0:T(1024)S(1)} %bitcast.64, s32[1024]{0:T(1024)S(1)} %iota.22, s32[]{:T(128)} %constant.13.clone.1), kind=kCustom, calls=%fused_computation.53 | custom fusion | bytes 200 | tf_op jit(solution)/shard_map/scatter | solution.py:44
  15.3 1.0 concatenate.6
  16.3 0.7 gather_fusion
  16.9 0.7 reshape.115
  17.6 6.3 %all-to-all-start = ((bf16[4,12,1024]{2,1,0:T(8,128)(2,1)}), bf16[4,12,1024]{2,1,0:T(8,128)(2,1)S(1)}, u32[]{:S(2)}, u32[]{:S(2)}) async-start(bf16[4,12,1024]{2,1,0:T(8,128)(2,1)} %reshape.115), calls=%async_computation | async-start | bytes 262144 | tf_op jit(solution)/shard_map/all_to_all | solution.py:64
  23.9 0.0 copy-done.4
  24.0 0.0 copy-done.6
  24.0 0.1 copy.21
  24.1 0.1 mul.62
  24.2 0.3 fusion
  24.5 1.5 %concatenate.7 = bf16[1025,1024]{1,0:T(8,128)(2,1)} pad(bf16[1024,1024]{1,0:T(8,128)(2,1)S(1)} %fusion, bf16[]{:T(256)} %constant.12.clone.1), padding=0_1x0_0 | pad | bytes 4196354 | tf_op jit(solution)/shard_map/concatenate | solution.py:52
  26.0 0.0 copy-start.1
  26.0 2.7 %gather_fusion.1 = bf16[48,1024]{1,0:T(8,128)(2,1)S(1)} fusion(bf16[1025,1024]{1,0:T(8,128)(2,1)} %concatenate.7, s32[1024]{0:T(1024)S(1)} %get-tuple-element.10), kind=kCustom, calls=%fused_computation.1 | custom fusion | bytes 196800 | tf_op jit(solution)/shard_map/gather | solution.py:53
  28.7 0.7 reshape.118
  29.4 0.6 all-to-all-done
  30.0 4.5 %all-to-all-start.2 = ((bf16[4,12,1024]{2,1,0:T(8,128)(2,1)}), bf16[4,12,1024]{2,1,0:T(8,128)(2,1)}, u32[]{:S(2)}, u32[]{:S(2)}) async-start(bf16[4,12,1024]{2,1,0:T(8,128)(2,1)} %reshape.118), calls=%async_computation.3 | async-start | bytes 262144 | tf_op jit(solution)/shard_map/all_to_all | solution.py:72
  34.5 0.0 reduce-scatter.6.cloned.1.call-start
  34.5 2.0 %all_gather.6 = bf16[4,12,2048]{2,1,0:T(8,128)(2,1)S(1)} all-gather(bf16[4,12,1024]{2,1,0:T(8,128)(2,1)S(1)} %all-to-all-done), channel_id=1, replica_groups=mesh['dp'=4,'expert'=4,'tensor'=2] {'tensor'}, dimensions={2}, use_global_device_ids=true | all-gather | bytes 294912 | tf_op jit(solution)/shard_map/all_gather | solution.py:10
  36.5 0.0 copy-done.1
  36.5 0.4 fusion.10
  36.9 0.0 copy-done
  36.9 1.0 multiply_convert_fusion.2
  37.9 2.7 %all-to-all-done.2 = bf16[4,12,1024]{2,1,0:T(8,128)(2,1)} async-done(((bf16[4,12,1024]{2,1,0:T(8,128)(2,1)}), bf16[4,12,1024]{2,1,0:T(8,128)(2,1)}, u32[]{:S(2)}, u32[]{:S(2)}) %all-to-all-start.2) | async-done | bytes 98336 | tf_op jit(solution)/shard_map/all_to_all | solution.py:72
  40.5 2.4 %all_gather.7 = bf16[4,12,2048]{2,1,0:T(8,128)(2,1)S(1)} all-gather(bf16[4,12,1024]{2,1,0:T(8,128)(2,1)} %all-to-all-done.2), channel_id=1, replica_groups=mesh['dp'=4,'expert'=4,'tensor'=2] {'tensor'}, dimensions={2}, use_global_device_ids=true | all-gather | bytes 294912 | tf_op jit(solution)/shard_map/all_gather | solution.py:10
  43.0 2.0 %fusion.2 = f32[4,12,384]{2,1,0:T(8,128)S(1)} fusion(bf16[4,12,2048]{2,1,0:T(8,128)(2,1)S(1)} %all_gather.7, bf16[1,384,2048]{2,1,0:T(8,128)(2,1)} %param.12), kind=kOutput, calls=%fused_computation.9 | convolution fusion | flops 75497472 | bytes 1843200 | tf_op jit(solution)/shard_map/ncd,fd->ncf/dot_general | solution.py:79
  45.0 0.0 copy-done.3
  45.0 0.6 fusion.8
  45.6 0.0 copy-start.2
  45.6 1.3 %fusion.1 = bf16[4,12,2048]{2,1,0:T(8,128)(2,1)} fusion(f32[4,12,2048]{2,1,0:T(8,128)S(1)} %fusion.8, bf16[1,2048,384]{2,1,0:T(8,128)(2,1)S(1)} %copy-done, f32[4,12,384]{2,1,0:T(8,128)S(1)} %fusion.2, f32[4,12,384]{2,1,0:T(8,128)S(1)} %fusion.10), kind=kOutput, calls=%fused_computation.7 | convolution fusion | flops 75804672 | bytes 2310144 | tf_op jit(solution)/shard_map/ncf,df->ncd/dot_general | solution.py:97
  46.9 0.0 reduce-scatter.6.cloned.1.call-update
  47.0 0.0 reduce-scatter.4.cloned.1.call-start
  47.0 0.0 copy-done.2
  47.0 1.1 %convolution_convert_fusion = bf16[4,12,2048]{2,1,0:T(8,128)(2,1)} fusion(bf16[4,12,384]{2,1,0:T(8,128)(2,1)S(1)} %get-tuple-element.8, bf16[1,384,2048]{2,1,0:T(8,128)(2,1)S(1)} %copy-done.2), kind=kOutput, calls=%fused_computation.8 | convolution fusion | flops 75595776 | bytes 1806336 | tf_op jit(solution)/shard_map/ncf,fd->ncd/dot_general | solution.py:69
  48.1 0.0 reduce-scatter.4.cloned.1.call-update
  48.1 0.0 reduce-scatter.8.cloned.1.call-start
  48.2 1.8 %bitcast_convert_fusion = bf16[384,2048]{1,0:T(8,128)(2,1)} fusion(bf16[4,12,384]{2,1,0:T(8,128)(2,1)S(1)} %get-tuple-element.8, bf16[4,12,2048]{2,1,0:T(8,128)(2,1)S(1)} %all_gather.7), kind=kOutput, calls=%fused_computation.5 | convolution fusion | flops 76283904 | bytes 1806336 | tf_op jit(solution)/shard_map/rf,rd->fd/dot_general | solution.py:91
  49.9 0.0 reduce-scatter.8.cloned.1.call-update
  50.0 3.9 %reduce-scatter.6.cloned.1.call-done = bf16[4,12,1024]{2,1,0:T(8,128)(2,1)} async-done(((bf16[4,12,2048]{2,1,0:T(8,128)(2,1)}), bf16[4,12,1024]{2,1,0:T(8,128)(2,1)}) %reduce-scatter.6.cloned.1.call-update) | async-done | bytes 98320 | tf_op jit(solution)/shard_map/reduce_scatter | solution.py:14
  53.8 4.8 %all-to-all-start.3 = ((bf16[4,12,1024]{2,1,0:T(8,128)(2,1)}), bf16[4,12,1024]{2,1,0:T(8,128)(2,1)S(1)}, u32[]{:S(2)}, u32[]{:S(2)}) async-start(bf16[4,12,1024]{2,1,0:T(8,128)(2,1)} %reduce-scatter.6.cloned.1.call-done), calls=%async_computation.5 | async-start | bytes 262144 | tf_op jit(solution)/shard_map/all_to_all | solution.py:20
  58.7 0.0 copy-done.5
  58.7 6.8 %reduce-scatter.4.cloned.1.call-done = bf16[4,12,1024]{2,1,0:T(8,128)(2,1)} async-done(((bf16[4,12,2048]{2,1,0:T(8,128)(2,1)}), bf16[4,12,1024]{2,1,0:T(8,128)(2,1)}) %reduce-scatter.4.cloned.1.call-update) | async-done | bytes 98320 | tf_op jit(solution)/shard_map/reduce_scatter | solution.py:14
  65.5 0.0 all-to-all-done.3
  65.5 4.9 %all-to-all-start.1 = ((bf16[4,12,1024]{2,1,0:T(8,128)(2,1)}), bf16[4,12,1024]{2,1,0:T(8,128)(2,1)S(1)}, u32[]{:S(2)}, u32[]{:S(2)}) async-start(bf16[4,12,1024]{2,1,0:T(8,128)(2,1)} %reduce-scatter.4.cloned.1.call-done), calls=%async_computation.2 | async-start | bytes 262144 | tf_op jit(solution)/shard_map/all_to_all | solution.py:20
  70.4 0.1 convert_reduce_fusion
  70.5 0.0 copy-done.7
  70.5 0.1 select_reduce_fusion
  70.6 6.2 %all-to-all-done.1 = bf16[4,12,1024]{2,1,0:T(8,128)(2,1)S(1)} async-done(((bf16[4,12,1024]{2,1,0:T(8,128)(2,1)}), bf16[4,12,1024]{2,1,0:T(8,128)(2,1)S(1)}, u32[]{:S(2)}, u32[]{:S(2)}) %all-to-all-start.1) | async-done | bytes 98336 | tf_op jit(solution)/shard_map/all_to_all | solution.py:20
  76.8 1.1 %convolution_convert_fusion.1 = bf16[128,1024]{1,0:T(8,128)(2,1)} fusion(f32[48,128]{1,0:T(8,128)S(1)} %convert_reduce_fusion, bf16[48,1024]{1,0:T(8,128)(2,1)S(1)} %reshape.119), kind=kOutput, calls=%fused_computation.19 | convolution fusion | flops 75628544 | bytes 385024 | tf_op jit(solution)/shard_map/dot_general | solution.py:101
  77.9 1.1 %convolution_convert_fusion.2 = bf16[128,1024]{1,0:T(8,128)(2,1)} fusion(f32[128,48]{0,1:T(8,128)S(1)} %select_reduce_fusion, bf16[48,1024]{1,0:T(8,128)(2,1)S(1)} %reshape.116), kind=kOutput, calls=%fused_computation.20 | convolution fusion | flops 75628544 | bytes 385024 | tf_op jit(solution)/shard_map/dot_general | solution.py:74
  79.1 22.2 %reduce-scatter.8.cloned.1.call-done = bf16[384,512]{1,0:T(8,128)(2,1)} async-done(((bf16[384,2048]{1,0:T(8,128)(2,1)}), bf16[384,512]{1,0:T(8,128)(2,1)}) %reduce-scatter.8.cloned.1.call-update) | async-done | bytes 393232 | tf_op jit(solution)/shard_map/reduce_scatter | solution.py:93
  (13 shorter events, 0.2 us)
Async XLA Ops:
  7.2 29.7 %copy-start = (bf16[1,2048,384]{2,1,0:T(8,128)(2,1)S(1)}, bf16[1,2048,384]{2,1,0:T(8,128)(2,1)}, u32[]{:S(2)}) copy-start(bf16[1,2048,384]{2,1,0:T(8,128)(2,1)} %param.11) | copy-start | bytes 4718596
  7.2 16.7 %copy-start.4 = (bf16[128,1024]{1,0:T(8,128)(2,1)S(1)}, bf16[128,1024]{1,0:T(8,128)(2,1)}, u32[]{:S(2)}) copy-start(bf16[128,1024]{1,0:T(8,128)(2,1)} %param.13) | copy-start | bytes 786436
  10.0 13.9 %copy-start.6 = (f32[128,8]{0,1:T(8,128)S(1)}, f32[128,8]{0,1:T(8,128)}, u32[]{:S(2)}) copy-start(f32[128,8]{0,1:T(8,128)} %param.9) | copy-start | bytes 12292
  17.6 12.4 %all-to-all-start = ((bf16[4,12,1024]{2,1,0:T(8,128)(2,1)}), bf16[4,12,1024]{2,1,0:T(8,128)(2,1)S(1)}, u32[]{:S(2)}, u32[]{:S(2)}) async-start(bf16[4,12,1024]{2,1,0:T(8,128)(2,1)} %reshape.115), calls=%async_computation | async-start | bytes 262144 | tf_op jit(solution)/shard_map/all_to_all | solution.py:64
  26.0 10.5 %copy-start.1 = (bf16[1,2048,384]{2,1,0:T(8,128)(2,1)S(1)}, bf16[1,2048,384]{2,1,0:T(8,128)(2,1)}, u32[]{:S(2)}) copy-start(bf16[1,2048,384]{2,1,0:T(8,128)(2,1)} %param.10) | copy-start | bytes 4718596
  30.0 10.5 %all-to-all-start.2 = ((bf16[4,12,1024]{2,1,0:T(8,128)(2,1)}), bf16[4,12,1024]{2,1,0:T(8,128)(2,1)}, u32[]{:S(2)}, u32[]{:S(2)}) async-start(bf16[4,12,1024]{2,1,0:T(8,128)(2,1)} %reshape.118), calls=%async_computation.3 | async-start | bytes 262144 | tf_op jit(solution)/shard_map/all_to_all | solution.py:72
  34.5 19.3 %reduce-scatter.6.cloned.1.call-start = ((), (), s32[]{:S(2)}) async-start(), calls=%async_computation.8 | async-start | bytes 393216 | tf_op jit(solution)/shard_map/reduce_scatter | solution.py:14
  40.5 4.4 %copy-start.3 = (f32[4,12,384]{2,1,0:T(8,128)S(1)}, f32[4,12,384]{2,1,0:T(8,128)}, u32[]{:S(2)}) copy-start(f32[4,12,384]{2,1,0:T(8,128)} %get-tuple-element.9) | copy-start | bytes 221188
  45.6 1.4 %copy-start.2 = (bf16[1,384,2048]{2,1,0:T(8,128)(2,1)S(1)}, bf16[1,384,2048]{2,1,0:T(8,128)(2,1)}, u32[]{:S(2)}) copy-start(bf16[1,384,2048]{2,1,0:T(8,128)(2,1)} %param.12) | copy-start | bytes 4718596
  47.0 18.6 %reduce-scatter.4.cloned.1.call-start = ((), (), s32[]{:S(2)}) async-start(), calls=%async_computation.7 | async-start | bytes 393216 | tf_op jit(solution)/shard_map/reduce_scatter | solution.py:14
  48.1 53.1 %reduce-scatter.8.cloned.1.call-start = ((), (), s32[]{:S(2)}) async-start(), calls=%async_computation.9 | async-start | bytes 1966080 | tf_op jit(solution)/shard_map/reduce_scatter | solution.py:93
  49.9 8.7 %copy-start.5 = (s32[128,8]{1,0:T(8,128)S(1)}, s32[128,8]{1,0:T(8,128)}, u32[]{:S(2)}) copy-start(s32[128,8]{1,0:T(8,128)} %get-tuple-element.3) | copy-start | bytes 12292
  49.9 20.5 %copy-start.7 = (f32[128,8]{0,1:T(8,128)S(1)}, f32[128,8]{0,1:T(8,128)}, u32[]{:S(2)}) copy-start(f32[128,8]{0,1:T(8,128)} %param.9) | copy-start | bytes 12292
  53.8 11.7 %all-to-all-start.3 = ((bf16[4,12,1024]{2,1,0:T(8,128)(2,1)}), bf16[4,12,1024]{2,1,0:T(8,128)(2,1)S(1)}, u32[]{:S(2)}, u32[]{:S(2)}) async-start(bf16[4,12,1024]{2,1,0:T(8,128)(2,1)} %reduce-scatter.6.cloned.1.call-done), calls=%async_computation.5 | async-start | bytes 262144 | tf_op jit(solution)/shard_map/all_to_all | solution.py:20
  65.5 11.2 %all-to-all-start.1 = ((bf16[4,12,1024]{2,1,0:T(8,128)(2,1)}), bf16[4,12,1024]{2,1,0:T(8,128)(2,1)S(1)}, u32[]{:S(2)}, u32[]{:S(2)}) async-start(bf16[4,12,1024]{2,1,0:T(8,128)(2,1)} %reduce-scatter.4.cloned.1.call-done), calls=%async_computation.2 | async-start | bytes 262144 | tf_op jit(solution)/shard_map/all_to_all | solution.py:20
Sparse Core Ops, SparseCore 0:
  47.1 6.7 reduce-scatter.5
  56.7 8.7 reduce-scatter.3
  69.1 32.0 reduce-scatter.7
where the time goes:
time: 108 us
  waiting for transfers between devices  42.3 us (39%)
  starting transfers between devices  20.6 us (19%)
  between operations  13.9 us (13%)
  local copies, waits for them, and re-layouts  13.5 us (12%)
  matrix products  10.4 us (10%)
  blocking collectives  4.4 us (4%)
  other arithmetic  2.58 us (2%)
    reduce_scatter x1, waiting for transfers between devices, per_device(): lax.psum_scatter(down_round.astype(jnp.bfloat16), 'dp', scatter_dimension...  22.2 us
    reduce_scatter x2, waiting for transfers between devices, tensor_total(): lax.psum_scatter(partial_value.astype(jnp.bfloat16), 'tensor', scatter_di...  10.7 us
    all_to_all x2, starting transfers between devices, return_rows(): lax.all_to_all(rows, 'expert', split_axis=0, concat_axis=0, tiled=True)  9.69 us
    all_to_all x1, starting transfers between devices, per_device(): lax.all_to_all(send_rows, 'expert', split_axis=0, concat_axis=0, tiled=True)  6.32 us
    all_to_all x2, waiting for transfers between devices, return_rows(): lax.all_to_all(rows, 'expert', split_axis=0, concat_axis=0, tiled=True)  6.2 us
    all_to_all x1, starting transfers between devices, per_device(): lax.all_to_all(grad_send, 'expert', split_axis=0, concat_axis=0, tiled=True)  4.51 us
    all_gather x2, blocking collectives, tensor_rows(): return lax.all_gather(rows, 'tensor', axis=2, tiled=True)  4.4 us
    scatter x1, local copies, waits for them, and re-layouts, per_device(): holder = jnp.full((slot_count + 1,), npairs, jnp.int32).at[target].set(jn...  4.3 us
  transfers between devices with their start and end apart: 7, of which 6 were waited for; matrix products, arithmetic and copies ran while one was open for 11% of the time, Pallas kernels for 0%

commit v1 on v0

v1 whole, which is shorter than its diff:
```python
import functools

import jax
import jax.numpy as jnp
from jax import lax
from jax.experimental import pallas as pl
from jax.experimental.pallas import tpu as pltpu
from jax.sharding import PartitionSpec as P

EXPERTS = 128
MESH = pl.DeviceIdType.MESH
BF = jnp.bfloat16
F32 = jnp.float32


def mm(a, b):
    return lax.dot_general(a, b, (((1,), (0,)), ((), ())), preferred_element_type=F32)


def mm_nt(a, b):
    return lax.dot_general(a, b, (((1,), (1,)), ((), ())), preferred_element_type=F32)


def mm_tn(a, b):
    return lax.dot_general(a, b, (((0,), (0,)), ((), ())), preferred_element_type=F32)


def kernel(
    dims,
    ids_ref, rw_ref, tok_hbm, cot_hbm, wg_hbm, wu_hbm, wd_hbm,
    mixed_hbm, tgrad_hbm, dgrad_hbm,
    tok, cot, wg, wu, wd, coll, comb, xs, gs, xr, gr, hd, gd,
    ps_o, ps_g, pr_o, pr_g, os, rs, ret_o, ret_g, mix, tgr, dgr,
    load_sem, out_sem,
    x_ss, x_rs, g_ss, g_rs, xf_ss, xf_rs, gf_ss, gf_rs,
    hd_ss, hd_rs, gd_ss, gd_rs, ex_ss, ex_rs, ro_ss, ro_rs, rg_ss, rg_rs,
):
    n_dp, n_ex, cap, fused = dims
    d = lax.axis_index("dp")
    s = lax.axis_index("expert")
    t = lax.axis_index("tensor")
    other = 1 - t
    n_tok, choose = ids_ref.shape
    half = tok.shape[1]
    rows = n_ex * cap
    lanes = coll.shape[1]
    blk = gd.shape[2]

    def ex_peer(k):
        return {"dp": d, "expert": lax.rem(s + k, n_ex), "tensor": t}

    def dp_peer(k):
        return {"dp": lax.rem(d + k, n_dp), "expert": s, "tensor": t}

    partner = {"dp": d, "expert": s, "tensor": other}

    def block(i):
        return pl.ds(pl.multiple_of(i * cap, cap), cap)

    def half_ds(i):
        return pl.ds(pl.multiple_of(i * half, half), half)

    def remote(src, dst, ss, rs_, dev):
        return pltpu.make_async_remote_copy(
            src_ref=src, dst_ref=dst, send_sem=ss, recv_sem=rs_, device_id=dev, device_id_type=MESH
        )

    loads = [
        pltpu.make_async_copy(a, b, load_sem.at[i])
        for i, (a, b) in enumerate(
            ((tok_hbm, tok), (cot_hbm, cot), (wg_hbm.at[0], wg), (wu_hbm.at[0], wu), (wd_hbm.at[0], wd))
        )
    ]
    for c in loads:
        c.start()

    barrier = pltpu.get_barrier_semaphore()
    peers = [ex_peer(k) for k in range(1, n_ex)] + [partner]
    if fused:
        peers += [dp_peer(k) for k in range(1, n_dp)]
    for p in peers:
        pl.semaphore_signal(barrier, inc=1, device_id=p, device_id_type=MESH)

    lane = lax.broadcasted_iota(jnp.int32, (n_tok, lanes), 1)
    e_lane = jnp.zeros((n_tok, lanes), jnp.int32)
    for n in range(1, n_ex):
        e_lane = e_lane + jnp.where(lane >= n * cap, 1, 0)
    c_lane = (lane - e_lane * cap).astype(F32)
    chosen = jnp.zeros((n_tok, lanes), F32)
    wsum = jnp.zeros((n_tok, lanes), F32)
    for k in range(choose):
        hit = ids_ref[:, k : k + 1] == e_lane
        chosen = chosen + jnp.where(hit, 1.0, 0.0)
        wsum = wsum + jnp.where(hit, rw_ref[:, k : k + 1], 0.0)
    later = lax.broadcasted_iota(jnp.int32, (n_tok, n_tok), 0) > lax.broadcasted_iota(
        jnp.int32, (n_tok, n_tok), 1
    )
    rank = mm(jnp.where(later, 1.0, 0.0).astype(BF), chosen.astype(BF))
    sel = jnp.where(rank == c_lane, chosen, 0.0)
    wsel = sel * wsum
    coll[...] = sel.astype(BF)
    w0 = wsel.astype(BF)
    r1 = wsel - w0.astype(F32)
    w1 = r1.astype(BF)
    comb[0] = w0
    comb[1] = w1
    comb[2] = (r1 - w1.astype(F32)).astype(BF)
    sel_t = sel.T[:rows].astype(BF)
    w_slot = jnp.sum(wsel.T[:rows], axis=1, keepdims=True)

    loads[0].wait()
    xs[...] = mm(sel_t, tok[...]).astype(BF)
    xr[t, block(s), :] = xs[block(s), :]

    pl.semaphore_wait(barrier, len(peers))

    def dispatch(src, dst, ss, rs_):
        out = []
        for k in range(1, n_ex):
            c = remote(
                src.at[block(lax.rem(s + k, n_ex))], dst.at[t, block(s)], ss.at[k - 1], rs_.at[k - 1], ex_peer(k)
            )
            c.start()
            out.append(c)
        return out

    def forwarder(dst, ss, rs_):
        out = []
        for k in range(n_ex):
            b = dst.at[t, block(lax.rem(s - k + n_ex, n_ex))]
            out.append(remote(b, b, ss.at[k], rs_.at[k], partner))
        return out

    x_send = dispatch(xs, xr, x_ss, x_rs)
    x_fwd = forwarder(xr, xf_ss, xf_rs)
    x_fwd[0].start()

    loads[1].wait()
    gs[...] = (mm(sel_t, cot[...]) * w_slot).astype(BF)
    gr[t, block(s), :] = gs[block(s), :]
    g_send = dispatch(gs, gr, g_ss, g_rs)
    g_fwd = forwarder(gr, gf_ss, gf_rs)
    g_fwd[0].start()

    for k in range(1, n_ex):
        x_send[k - 1].wait_recv()
        x_fwd[k].start()
    loads[2].wait()
    loads[3].wait()
    gate = mm(xr[t], wg[half_ds(t), :])
    up = mm(xr[t], wu[half_ds(t), :])
    for c in x_fwd:
        c.wait_recv()
    gate = gate + mm(xr[other], wg[half_ds(other), :])
    up = up + mm(xr[other], wu[half_ds(other), :])
    sig = jax.nn.sigmoid(gate)
    act = gate * sig
    hidden = (act * up).astype(BF)
    hd[d] = hidden
    hd_send = []
    gd_send = []
    if fused:
        for k in range(1, n_dp):
            c = remote(hd.at[d], hd.at[d], hd_ss.at[k - 1], hd_rs.at[k - 1], dp_peer(k))
            c.start()
            hd_send.append(c)

    loads[4].wait()
    ps_o[...] = mm(hidden, wd[:, half_ds(other)]).astype(BF)
    ex_o = remote(ps_o, pr_o, ex_ss.at[0], ex_rs.at[0], partner)
    ex_o.start()
    for k in range(1, n_ex):
        g_send[k - 1].wait_recv()
        g_fwd[k].start()
    own_o = mm(hidden, wd[:, half_ds(t)]).astype(BF).astype(F32)

    def give_back(src, dst, ss, rs_):
        out = []
        for k in range(1, n_ex):
            c = remote(
                src.at[block(lax.rem(s + k, n_ex))], dst.at[block(s)], ss.at[k - 1], rs_.at[k - 1], ex_peer(k)
            )
            c.start()
            out.append(c)
        dst[block(s), :] = src[block(s), :]
        return out

    ex_o.wait_recv()
    os[...] = (own_o + pr_o[...].astype(F32)).astype(BF)
    ro_send = give_back(os, ret_o, ro_ss, ro_rs)

    hgrad = mm_nt(gr[t], wd[:, half_ds(t)])
    for c in g_fwd:
        c.wait_recv()
    if fused:
        for k in range(1, n_dp):
            at = lax.rem(d + k, n_dp) * blk
            c = remote(
                gr.at[at // half, :, pl.ds(pl.multiple_of(lax.rem(at, half), blk), blk)],
                gd.at[d],
                gd_ss.at[k - 1],
                gd_rs.at[k - 1],
                dp_peer(k),
            )
            c.start()
            gd_send.append(c)
    hgrad = hgrad + mm_nt(gr[other], wd[:, half_ds(other)])
    gate_term = (hgrad * up * sig * (1.0 + gate * (1.0 - sig))).astype(BF)
    up_term = (hgrad * act).astype(BF)

    ps_g[...] = (
        mm_nt(gate_term, wg[half_ds(other), :]) + mm_nt(up_term, wu[half_ds(other), :])
    ).astype(BF)
    ex_g = remote(ps_g, pr_g, ex_ss.at[1], ex_rs.at[1], partner)
    ex_g.start()
    own_g = (
        (mm_nt(gate_term, wg[half_ds(t), :]) + mm_nt(up_term, wu[half_ds(t), :])).astype(BF).astype(F32)
    )
    ex_g.wait_recv()
    rs[...] = (own_g + pr_g[...].astype(F32)).astype(BF)
    rg_send = give_back(rs, ret_g, rg_ss, rg_rs)

    for c in ro_send:
        c.wait_recv()
    ro = ret_o[...]
    mix[...] = (
        mm(comb[0, :, :rows], ro) + mm(comb[1, :, :rows], ro) + mm(comb[2, :, :rows], ro)
    ).astype(BF)
    out_m = pltpu.make_async_copy(mix, mixed_hbm, out_sem.at[0])
    out_m.start()

    if fused:
        at = d * blk
        total = mm_tn(
            hd[d], gr[at // half, :, pl.ds(pl.multiple_of(lax.rem(at, half), blk), blk)]
        ).astype(BF).astype(F32)
        for k in range(1, n_dp):
            hd_send[k - 1].wait_recv()
            gd_send[k - 1].wait_recv()
            src = lax.rem(d - k + n_dp, n_dp)
            total = total + mm_tn(hd[src], gd[src]).astype(BF).astype(F32)
        dgr[...] = total.astype(BF)
    else:
        for i in range(2):
            dgr[:, i * half : (i + 1) * half] = mm_tn(hidden, gr[i]).astype(BF)
    out_d = pltpu.make_async_copy(dgr, dgrad_hbm, out_sem.at[1])
    out_d.start()

    for c in rg_send:
        c.wait_recv()
    tgr[...] = mm(coll[:, :rows], ret_g[...]).astype(BF)
    out_t = pltpu.make_async_copy(tgr, tgrad_hbm, out_sem.at[2])
    out_t.start()

    for c in x_send + g_send + x_fwd + g_fwd + hd_send + gd_send + [ex_o, ex_g] + ro_send + rg_send:
        c.wait_send()
    out_m.wait()
    out_d.wait()
    out_t.wait()


def per_device(n_dp, n_ex, tokens, expert_ids, route_weight, gate_weight, up_weight, down_weight, cotangent):
    n_tok, choose = expert_ids.shape
    capacity = 3 * n_tok * choose // (2 * EXPERTS)
    cap = -(-capacity // 16) * 16
    half = tokens.shape[1]
    full = gate_weight.shape[1]
    width = gate_weight.shape[2]
    rows = n_ex * cap
    lanes = -(-rows // 128) * 128
    blk = full // n_dp
    fused = blk % 128 == 0
    d_cols = blk if fused else full
    slots = n_dp if fused else n_dp
    gd_cols = blk if fused else 128
    vm = pltpu.VMEM
    dma = pltpu.SemaphoreType.DMA
    ne, nd = n_ex - 1, max(n_dp - 1, 1)
    hbm = pl.BlockSpec(memory_space=pl.ANY)
    inv = pl.BlockSpec(memory_space=pltpu.VMEM)
    mixed, token_grad, down = pl.pallas_call(
        functools.partial(kernel, (n_dp, n_ex, cap, fused)),
        out_shape=(
            jax.ShapeDtypeStruct((n_tok, half), BF),
            jax.ShapeDtypeStruct((n_tok, half), BF),
            jax.ShapeDtypeStruct((width, d_cols), BF),
        ),
        in_specs=[inv, inv, hbm, hbm, hbm, hbm, hbm],
        out_specs=(hbm, hbm, hbm),
        scratch_shapes=[
            vm((n_tok, half), BF), vm((n_tok, half), BF),
            vm((full, width), BF), vm((full, width), BF), vm((width, full), BF),
            vm((n_tok, lanes), BF), vm((3, n_tok, lanes), BF),
            vm((rows, half), BF), vm((rows, half), BF),
            vm((2, rows, half), BF), vm((2, rows, half), BF),
            vm((slots, rows, width), BF), vm((slots, rows, gd_cols), BF),
            vm((rows, half), BF), vm((rows, half), BF), vm((rows, half), BF), vm((rows, half), BF),
            vm((rows, half), BF), vm((rows, half), BF), vm((rows, half), BF), vm((rows, half), BF),
            vm((n_tok, half), BF), vm((n_tok, half), BF), vm((width, d_cols), BF),
            dma((5,)), dma((3,)),
            dma((ne,)), dma((ne,)), dma((ne,)), dma((ne,)),
            dma((n_ex,)), dma((n_ex,)), dma((n_ex,)), dma((n_ex,)),
            dma((nd,)), dma((nd,)), dma((nd,)), dma((nd,)),
            dma((2,)), dma((2,)),
            dma((ne,)), dma((ne,)), dma((ne,)), dma((ne,)),
        ],
        compiler_params=pltpu.CompilerParams(
            collective_id=0, has_side_effects=True, vmem_limit_bytes=56 * 1024 * 1024
        ),
    )(expert_ids, route_weight, tokens, cotangent, gate_weight, up_weight, down_weight)
    if not fused:
        down = lax.psum_scatter(down, "dp", scatter_dimension=1, tiled=True)
    return mixed, token_grad, down[None]


def solution(mesh):
    placed = (
        P(("dp", "expert"), "tensor"),
        P(("dp", "expert"), None),
        P(("dp", "expert"), None),
        P("expert", None, "tensor"),
        P("expert", None, "tensor"),
        P("expert", "tensor", None),
        P(("dp", "expert"), "tensor"),
    )
    return jax.shard_map(
        functools.partial(per_device, mesh.shape["dp"], mesh.shape["expert"]),
        mesh=mesh,
        in_specs=placed,
        out_specs=(
            P(("dp", "expert"), "tensor"),
            P(("dp", "expert"), "tensor"),
            P("expert", "tensor", "dp"),
        ),
        check_vma=False,
    )
```

time: 108 us -> 31.8 us (0.29)
  waiting for transfers between devices: 42.3 us -> 0 us
  Pallas kernels: 0 us -> 22.9 us
  starting transfers between devices: 20.6 us -> 0 us
  between operations: 13.9 us -> 0.64 us
  matrix products: 10.4 us -> 0 us
  local copies, waits for them, and re-layouts: 13.5 us -> 7.94 us
  blocking collectives: 4.4 us -> 0 us
  other arithmetic: 2.58 us -> 0 us
    reduce_scatter x3 -> x0, waiting for transfers between devices: 32.9 us -> none  [the longest x1 22.2 us: per_device(): lax.psum_scatter(down_round.astype(jnp.bfloat16), 'dp', scatter_dimension...]
    pallas_call x0 -> x1, Pallas kernels: none -> 22.9 us  [per_device(): pl.pallas_call(functools.partial(kernel, (n_dp, n_ex, cap, fused)), out_s...]
    all_to_all x4 -> x0, starting transfers between devices: 20.5 us -> none  [the longest x2 9.69 us: return_rows(): lax.all_to_all(rows, 'expert', split_axis=0, concat_axis=0, tiled=True)]
    dot_general x9 -> x0, matrix products: 10.4 us -> none  [the longest x1 2 us: per_device(): jnp.einsum('ncd,fd->ncf', grad_full, w_down, preferred_element_type=jnp.f...]
    all_to_all x4 -> x0, waiting for transfers between devices: 9.43 us -> none  [the longest x2 6.2 us: return_rows(): lax.all_to_all(rows, 'expert', split_axis=0, concat_axis=0, tiled=True)]
    unnamed x18 -> x5, local copies, waits for them, and re-layouts: 1.07 us -> 7.94 us
    all_gather x2 -> x0, blocking collectives: 4.4 us -> none  [tensor_rows(): return lax.all_gather(rows, 'tensor', axis=2, tiled=True)]
    scatter x1 -> x0, local copies, waits for them, and re-layouts: 4.3 us -> none  [per_device(): holder = jnp.full((slot_count + 1,), npairs, jnp.int32).at[target].set(jn...]
  transfers between devices with their start and end apart: 7 -> 0, of which waited for: 6 -> 0; matrix products, arithmetic and copies ran while one was open for 11% -> 0% of each run, Pallas kernels for 0% -> 0%
where the time goes in v1:
time: 31.8 us; the launch traced here: 31.5 us
  Pallas kernels  22.9 us (72%)
  local copies, waits for them, and re-layouts  7.94 us (25%)
  between operations  0.64 us (2%)
    pallas_call x1, Pallas kernels, per_device(): pl.pallas_call(functools.partial(kernel, (n_dp, n_ex, cap, fused)), out_s...  22.9 us
    unnamed x5, local copies, waits for them, and re-layouts  7.94 us

profile of v1, /device:TPU:0, one launch (start us, length us, event | category | flops | bytes accessed | tf_op | source)
XLA Modules:
  0.0 31.5 jit_solution(14711764632455021673)
XLA Ops:
  0.6 1.4 %copy.10.ids_ref = s32[128,8]{1,0:T(8,128)} copy(s32[128,8]{0,1:T(8,128)} %param.8) | data formatting | bytes 8192 | tf_op args[1]
  2.0 1.4 %copy.11.rw_ref = f32[128,8]{1,0:T(8,128)} copy(f32[128,8]{0,1:T(8,128)} %param.9) | data formatting | bytes 8192 | tf_op args[2]
  3.5 22.9 %shard_map.94 = (bf16[128,1024]{1,0:T(8,128)(2,1)}, bf16[128,1024]{1,0:T(8,128)(2,1)}, bf16[384,512]{1,0:T(8,128)(2,1)}) custom-call(s32[128,8]{1,0:T(8,128)} %copy.10.ids_ref, f32[128,8]{1,0:T(8,128)} %copy.11.rw_ref, bf16[128,1024]{1,0:T(8,128)(2,1)} %tok_hbm.1, bf16[128,1024]{1,0:T(8,128)(2,1)} %cot_hbm.1, bf16[1,2048,384]{2,1,0:T(8,128)(2,1)} %wg_hbm.1, ...), custom_call_target="tpu_custom_call" | custom-call | tf_op jit(solution)/shard_map/pallas_call | solution.py:281
  26.4 1.7 %copy.15 = bf16[128,1024]{1,0:T(8,128)(2,1)} copy(bf16[128,1024]{1,0:T(8,128)(2,1)} %get-tuple-element.12) | data formatting | bytes 524288
  28.0 1.7 %copy.16 = bf16[128,1024]{1,0:T(8,128)(2,1)} copy(bf16[128,1024]{1,0:T(8,128)(2,1)} %get-tuple-element.13) | data formatting | bytes 524288
  29.7 1.8 %copy.17 = bf16[1,384,512]{2,1,0:T(8,128)(2,1)} copy(bf16[1,384,512]{2,1,0:T(8,128)(2,1)} %bitcast.1) | data formatting | bytes 786432

commit v2 on v1

--- a/solution.py
+++ b/solution.py
@@ -28,10 +28,10 @@
 def kernel(
     dims,
     ids_ref, rw_ref, tok_hbm, cot_hbm, wg_hbm, wu_hbm, wd_hbm,
-    mixed_hbm, tgrad_hbm, dgrad_hbm,
+    mix, tgr, dgr,
     tok, cot, wg, wu, wd, coll, comb, xs, gs, xr, gr, hd, gd,
-    ps_o, ps_g, pr_o, pr_g, os, rs, ret_o, ret_g, mix, tgr, dgr,
-    load_sem, out_sem,
+    ps_o, ps_g, pr_o, pr_g, os, rs, ret_o, ret_g,
+    load_sem,
     x_ss, x_rs, g_ss, g_rs, xf_ss, xf_rs, gf_ss, gf_rs,
     hd_ss, hd_rs, gd_ss, gd_rs, ex_ss, ex_rs, ro_ss, ro_rs, rg_ss, rg_rs,
 ):
@@ -40,10 +40,9 @@
     s = lax.axis_index("expert")
     t = lax.axis_index("tensor")
     other = 1 - t
-    n_tok, choose = ids_ref.shape
+    choose, n_tok = ids_ref.shape
     half = tok.shape[1]
     rows = n_ex * cap
-    lanes = coll.shape[1]
     blk = gd.shape[2]
 
     def ex_peer(k):
@@ -81,32 +80,25 @@
     for p in peers:
         pl.semaphore_signal(barrier, inc=1, device_id=p, device_id_type=MESH)
 
-    lane = lax.broadcasted_iota(jnp.int32, (n_tok, lanes), 1)
-    e_lane = jnp.zeros((n_tok, lanes), jnp.int32)
+    row = lax.broadcasted_iota(jnp.int32, (rows, n_tok), 0)
+    e_row = jnp.zeros((rows, n_tok), jnp.int32)
     for n in range(1, n_ex):
-        e_lane = e_lane + jnp.where(lane >= n * cap, 1, 0)
-    c_lane = (lane - e_lane * cap).astype(F32)
-    chosen = jnp.zeros((n_tok, lanes), F32)
-    wsum = jnp.zeros((n_tok, lanes), F32)
+        e_row = e_row + jnp.where(row >= n * cap, 1, 0)
+    c_row = (row - e_row * cap).astype(F32)
+    chosen = jnp.zeros((rows, n_tok), F32)
+    wsum = jnp.zeros((rows, n_tok), F32)
     for k in range(choose):
-        hit = ids_ref[:, k : k + 1] == e_lane
+        hit = ids_ref[k : k + 1, :] == e_row
         chosen = chosen + jnp.where(hit, 1.0, 0.0)
-        wsum = wsum + jnp.where(hit, rw_ref[:, k : k + 1], 0.0)
-    later = lax.broadcasted_iota(jnp.int32, (n_tok, n_tok), 0) > lax.broadcasted_iota(
+        wsum = wsum + jnp.where(hit, rw_ref[k : k + 1, :], 0.0)
+    earlier = lax.broadcasted_iota(jnp.int32, (n_tok, n_tok), 0) < lax.broadcasted_iota(
         jnp.int32, (n_tok, n_tok), 1
     )
-    rank = mm(jnp.where(later, 1.0, 0.0).astype(BF), chosen.astype(BF))
-    sel = jnp.where(rank == c_lane, chosen, 0.0)
+    rank = mm(chosen.astype(BF), jnp.where(earlier, 1.0, 0.0).astype(BF))
+    sel = jnp.where(rank == c_row, chosen, 0.0)
     wsel = sel * wsum
-    coll[...] = sel.astype(BF)
-    w0 = wsel.astype(BF)
-    r1 = wsel - w0.astype(F32)
-    w1 = r1.astype(BF)
-    comb[0] = w0
-    comb[1] = w1
-    comb[2] = (r1 - w1.astype(F32)).astype(BF)
-    sel_t = sel.T[:rows].astype(BF)
-    w_slot = jnp.sum(wsel.T[:rows], axis=1, keepdims=True)
+    sel_t = sel.astype(BF)
+    w_slot = jnp.sum(wsel, axis=1, keepdims=True)
 
     loads[0].wait()
     xs[...] = mm(sel_t, tok[...]).astype(BF)
@@ -141,6 +133,15 @@
     g_send = dispatch(gs, gr, g_ss, g_rs)
     g_fwd = forwarder(gr, gf_ss, gf_rs)
     g_fwd[0].start()
+
+    coll[...] = sel.T.astype(BF)
+    wcol = wsel.T
+    w0 = wcol.astype(BF)
+    r1 = wcol - w0.astype(F32)
+    w1 = r1.astype(BF)
+    comb[0] = w0
+    comb[1] = w1
+    comb[2] = (r1 - w1.astype(F32)).astype(BF)
 
     for k in range(1, n_ex):
         x_send[k - 1].wait_recv()
@@ -224,10 +225,8 @@
         c.wait_recv()
     ro = ret_o[...]
     mix[...] = (
-        mm(comb[0, :, :rows], ro) + mm(comb[1, :, :rows], ro) + mm(comb[2, :, :rows], ro)
+        mm(comb[0], ro) + mm(comb[1], ro) + mm(comb[2], ro)
     ).astype(BF)
-    out_m = pltpu.make_async_copy(mix, mixed_hbm, out_sem.at[0])
-    out_m.start()
 
     if fused:
         at = d * blk
@@ -243,20 +242,24 @@
     else:
         for i in range(2):
             dgr[:, i * half : (i + 1) * half] = mm_tn(hidden, gr[i]).astype(BF)
-    out_d = pltpu.make_async_copy(dgr, dgrad_hbm, out_sem.at[1])
-    out_d.start()
 
     for c in rg_send:
         c.wait_recv()
-    tgr[...] = mm(coll[:, :rows], ret_g[...]).astype(BF)
-    out_t = pltpu.make_async_copy(tgr, tgrad_hbm, out_sem.at[2])
-    out_t.start()
+    tgr[...] = mm(coll[...], ret_g[...]).astype(BF)
 
     for c in x_send + g_send + x_fwd + g_fwd + hd_send + gd_send + [ex_o, ex_g] + ro_send + rg_send:
         c.wait_send()
-    out_m.wait()
-    out_d.wait()
-    out_t.wait()
+
+
+def write_kernel(a, b, c, a_out, b_out, c_out, sem):
+    copies = [
+        pltpu.make_async_copy(i, o, sem.at[k])
+        for k, (i, o) in enumerate(((a, a_out), (b, b_out), (c, c_out)))
+    ]
+    for cp in copies:
+        cp.start()
+    for cp in copies:
+        cp.wait()
 
 
 def per_device(n_dp, n_ex, tokens, expert_ids, route_weight, gate_weight, up_weight, down_weight, cotangent):
@@ -267,7 +270,6 @@
     full = gate_weight.shape[1]
     width = gate_weight.shape[2]
     rows = n_ex * cap
-    lanes = -(-rows // 128) * 128
     blk = full // n_dp
     fused = blk % 128 == 0
     d_cols = blk if fused else full
@@ -280,24 +282,19 @@
     inv = pl.BlockSpec(memory_space=pltpu.VMEM)
     mixed, token_grad, down = pl.pallas_call(
         functools.partial(kernel, (n_dp, n_ex, cap, fused)),
-        out_shape=(
-            jax.ShapeDtypeStruct((n_tok, half), BF),
-            jax.ShapeDtypeStruct((n_tok, half), BF),
-            jax.ShapeDtypeStruct((width, d_cols), BF),
-        ),
+        out_shape=(vm((n_tok, half), BF), vm((n_tok, half), BF), vm((width, d_cols), BF)),
         in_specs=[inv, inv, hbm, hbm, hbm, hbm, hbm],
-        out_specs=(hbm, hbm, hbm),
+        out_specs=(inv, inv, inv),
         scratch_shapes=[
             vm((n_tok, half), BF), vm((n_tok, half), BF),
             vm((full, width), BF), vm((full, width), BF), vm((width, full), BF),
-            vm((n_tok, lanes), BF), vm((3, n_tok, lanes), BF),
+            vm((n_tok, rows), BF), vm((3, n_tok, rows), BF),
             vm((rows, half), BF), vm((rows, half), BF),
             vm((2, rows, half), BF), vm((2, rows, half), BF),
             vm((slots, rows, width), BF), vm((slots, rows, gd_cols), BF),
             vm((rows, half), BF), vm((rows, half), BF), vm((rows, half), BF), vm((rows, half), BF),
             vm((rows, half), BF), vm((rows, half), BF), vm((rows, half), BF), vm((rows, half), BF),
-            vm((n_tok, half), BF), vm((n_tok, half), BF), vm((width, d_cols), BF),
-            dma((5,)), dma((3,)),
+            dma((5,)),
             dma((ne,)), dma((ne,)), dma((ne,)), dma((ne,)),
             dma((n_ex,)), dma((n_ex,)), dma((n_ex,)), dma((n_ex,)),
             dma((nd,)), dma((nd,)), dma((nd,)), dma((nd,)),
@@ -307,7 +304,14 @@
         compiler_params=pltpu.CompilerParams(
             collective_id=0, has_side_effects=True, vmem_limit_bytes=56 * 1024 * 1024
         ),
-    )(expert_ids, route_weight, tokens, cotangent, gate_weight, up_weight, down_weight)
+    )(expert_ids.T, route_weight.T, tokens, cotangent, gate_weight, up_weight, down_weight)
+    mixed, token_grad, down = pl.pallas_call(
+        write_kernel,
+        out_shape=tuple(jax.ShapeDtypeStruct(a.shape, BF) for a in (mixed, token_grad, down)),
+        in_specs=[inv, inv, inv],
+        out_specs=(hbm, hbm, hbm),
+        scratch_shapes=[dma((3,))],
+    )(*(pltpu.with_memory_space_constraint(a, pltpu.VMEM) for a in (mixed, token_grad, down)))
     if not fused:
         down = lax.psum_scatter(down, "dp", scatter_dimension=1, tiled=True)
     return mixed, token_grad, down[None]

time: 31.8 us -> 23.9 us (0.75)
  local copies, waits for them, and re-layouts: 7.94 us -> 0 us
    unnamed x5 -> x0, local copies, waits for them, and re-layouts: 7.94 us -> none
    pallas_call x0 -> x1, Pallas kernels: none -> 0.95 us  [per_device(): pl.pallas_call(write_kernel, out_shape=tuple((jax.ShapeDtypeStruct(a.shap...]
    pallas_call x1, Pallas kernels: 22.9 us -> 22.1 us  [per_device(): pl.pallas_call(functools.partial(kernel, (n_dp, n_ex, cap, fused)), out_s...]
where the time goes in v2:
time: 23.9 us; the launch traced here: 23.7 us
  Pallas kernels  23 us (96%)
  between operations  0.64 us (3%)
    pallas_call x1, Pallas kernels, per_device(): pl.pallas_call(functools.partial(kernel, (n_dp, n_ex, cap, fused)), out_s...  22.1 us
    pallas_call x1, Pallas kernels, per_device(): pl.pallas_call(write_kernel, out_shape=tuple((jax.ShapeDtypeStruct(a.shap...  0.95 us

profile of v2, /device:TPU:0, one launch (start us, length us, event | category | flops | bytes accessed | tf_op | source)
XLA Modules:
  0.0 23.7 jit_solution(3978021496518900319)
XLA Ops:
  0.6 22.1 %shard_map.94 = (bf16[128,1024]{1,0:T(8,128)(2,1)S(1)}, bf16[128,1024]{1,0:T(8,128)(2,1)S(1)}, bf16[384,512]{1,0:T(8,128)(2,1)S(1)}) custom-call(s32[8,128]{1,0:T(8,128)} %bitcast.3, f32[8,128]{1,0:T(8,128)} %bitcast.4, bf16[128,1024]{1,0:T(8,128)(2,1)} %tok_hbm.1, bf16[128,1024]{1,0:T(8,128)(2,1)} %cot_hbm.1, bf16[1,2048,384]{2,1,0:T(8,128)(2,1)} %wg_hbm.1, ...), custom_call_target="tpu_custom_call" | custom-call | tf_op jit(solution)/shard_map/pallas_call | solution.py:283
  22.7 0.9 %shard_map.95 = (bf16[128,1024]{1,0:T(8,128)(2,1)}, bf16[128,1024]{1,0:T(8,128)(2,1)}, bf16[384,512]{1,0:T(8,128)(2,1)}) custom-call(bf16[128,1024]{1,0:T(8,128)(2,1)S(1)} %get-tuple-element.9.a, bf16[128,1024]{1,0:T(8,128)(2,1)S(1)} %get-tuple-element.10.b, bf16[384,512]{1,0:T(8,128)(2,1)S(1)} %get-tuple-element.11.c), custom_call_target="tpu_custom_call" | custom-call | tf_op jit(solution)/shard_map/pallas_call | solution.py:308

commit v3 on v2

--- a/solution.py
+++ b/solution.py
@@ -29,13 +29,13 @@
     dims,
     ids_ref, rw_ref, tok_hbm, cot_hbm, wg_hbm, wu_hbm, wd_hbm,
     mix, tgr, dgr,
-    tok, cot, wg, wu, wd, coll, comb, xs, gs, xr, gr, hd, gd,
+    tok, cot, wg, wu, wd, coll, comb, xs, gs, xp, gp, xr, gr, hd, gd,
     ps_o, ps_g, pr_o, pr_g, os, rs, ret_o, ret_g,
     load_sem,
     x_ss, x_rs, g_ss, g_rs, xf_ss, xf_rs, gf_ss, gf_rs,
     hd_ss, hd_rs, gd_ss, gd_rs, ex_ss, ex_rs, ro_ss, ro_rs, rg_ss, rg_rs,
 ):
-    n_dp, n_ex, cap, fused = dims
+    n_dp, n_ex, cap, capacity, parts, piece, fused = dims
     d = lax.axis_index("dp")
     s = lax.axis_index("expert")
     t = lax.axis_index("tensor")
@@ -100,9 +100,48 @@
     sel_t = sel.astype(BF)
     w_slot = jnp.sum(wsel, axis=1, keepdims=True)
 
+    sel_x, w_x, back = [], [], []
+    if parts:
+        r_sq = lax.broadcasted_iota(jnp.int32, (rows, rows), 0)
+        m_sq = lax.broadcasted_iota(jnp.int32, (rows, rows), 1)
+        base = jnp.zeros((rows, rows), jnp.int32)
+        for n in range(1, n_ex):
+            base = base + jnp.where(m_sq >= n * cap, cap, 0)
+        m_c = m_sq - base
+        back.append(jnp.where((r_sq == m_sq) & (m_c < capacity), 1.0, 0.0).astype(BF))
+        c_int = row - e_row * cap
+        for i in range(parts):
+            c_i = jnp.where(c_int >= capacity, (c_int - capacity) * parts + i, -1).astype(F32)
+            s_i = jnp.where(rank == c_i, chosen, 0.0)
+            sel_x.append(s_i.astype(BF))
+            w_x.append(jnp.sum(s_i * wsum, axis=1, keepdims=True))
+            place = base + (m_c - capacity) * parts + i
+            back.append(jnp.where((m_c >= capacity) & (r_sq == place), 1.0, 0.0).astype(BF))
+
+    def pack(src, dst, weighted):
+        if not parts:
+            v = mm(sel_t, src[...])
+            dst[...] = (v * w_slot if weighted else v).astype(BF)
+        for i in range(parts):
+            here = slice(i * piece, (i + 1) * piece)
+            a = mm(sel_t, src[:, here])
+            b = mm(sel_x[i], src[:, parts * piece :])
+            dst[:, here] = (a * w_slot + b * w_x[i] if weighted else a + b).astype(BF)
+
+    def unpack(src, dst, h):
+        v = src[h]
+        if not parts:
+            dst[h] = v
+        else:
+            dst[h, :, : parts * piece] = mm(back[0], v).astype(BF)
+            tail = mm(back[1], v[:, :piece])
+            for i in range(1, parts):
+                tail = tail + mm(back[i + 1], v[:, i * piece : (i + 1) * piece])
+            dst[h, :, parts * piece :] = tail.astype(BF)
+
     loads[0].wait()
-    xs[...] = mm(sel_t, tok[...]).astype(BF)
-    xr[t, block(s), :] = xs[block(s), :]
+    pack(tok, xs, False)
+    xp[t, block(s), :] = xs[block(s), :]
 
     pl.semaphore_wait(barrier, len(peers))
 
@@ -123,15 +162,15 @@
             out.append(remote(b, b, ss.at[k], rs_.at[k], partner))
         return out
 
-    x_send = dispatch(xs, xr, x_ss, x_rs)
-    x_fwd = forwarder(xr, xf_ss, xf_rs)
+    x_send = dispatch(xs, xp, x_ss, x_rs)
+    x_fwd = forwarder(xp, xf_ss, xf_rs)
     x_fwd[0].start()
 
     loads[1].wait()
-    gs[...] = (mm(sel_t, cot[...]) * w_slot).astype(BF)
-    gr[t, block(s), :] = gs[block(s), :]
-    g_send = dispatch(gs, gr, g_ss, g_rs)
-    g_fwd = forwarder(gr, gf_ss, gf_rs)
+    pack(cot, gs, True)
+    gp[t, block(s), :] = gs[block(s), :]
+    g_send = dispatch(gs, gp, g_ss, g_rs)
+    g_fwd = forwarder(gp, gf_ss, gf_rs)
     g_fwd[0].start()
 
     coll[...] = sel.T.astype(BF)
@@ -146,12 +185,14 @@
     for k in range(1, n_ex):
         x_send[k - 1].wait_recv()
         x_fwd[k].start()
+    unpack(xp, xr, t)
     loads[2].wait()
     loads[3].wait()
     gate = mm(xr[t], wg[half_ds(t), :])
     up = mm(xr[t], wu[half_ds(t), :])
     for c in x_fwd:
         c.wait_recv()
+    unpack(xp, xr, other)
     gate = gate + mm(xr[other], wg[half_ds(other), :])
     up = up + mm(xr[other], wu[half_ds(other), :])
     sig = jax.nn.sigmoid(gate)
@@ -186,6 +227,7 @@
         dst[block(s), :] = src[block(s), :]
         return out
 
+    unpack(gp, gr, t)
     ex_o.wait_recv()
     os[...] = (own_o + pr_o[...].astype(F32)).astype(BF)
     ro_send = give_back(os, ret_o, ro_ss, ro_rs)
@@ -193,6 +235,7 @@
     hgrad = mm_nt(gr[t], wd[:, half_ds(t)])
     for c in g_fwd:
         c.wait_recv()
+    unpack(gp, gr, other)
     if fused:
         for k in range(1, n_dp):
             at = lax.rem(d + k, n_dp) * blk
@@ -270,6 +313,12 @@
     full = gate_weight.shape[1]
     width = gate_weight.shape[2]
     rows = n_ex * cap
+    spare = cap - capacity
+    parts = capacity // spare if spare and capacity % spare == 0 else 0
+    if parts and half % ((parts + 1) * 128):
+        parts = 0
+    piece = half // (parts + 1)
+    wide = parts * piece if parts else half
     blk = full // n_dp
     fused = blk % 128 == 0
     d_cols = blk if fused else full
@@ -281,7 +330,7 @@
     hbm = pl.BlockSpec(memory_space=pl.ANY)
     inv = pl.BlockSpec(memory_space=pltpu.VMEM)
     mixed, token_grad, down = pl.pallas_call(
-        functools.partial(kernel, (n_dp, n_ex, cap, fused)),
+        functools.partial(kernel, (n_dp, n_ex, cap, capacity, parts, piece, fused)),
         out_shape=(vm((n_tok, half), BF), vm((n_tok, half), BF), vm((width, d_cols), BF)),
         in_specs=[inv, inv, hbm, hbm, hbm, hbm, hbm],
         out_specs=(inv, inv, inv),
@@ -289,7 +338,8 @@
             vm((n_tok, half), BF), vm((n_tok, half), BF),
             vm((full, width), BF), vm((full, width), BF), vm((width, full), BF),
             vm((n_tok, rows), BF), vm((3, n_tok, rows), BF),
-            vm((rows, half), BF), vm((rows, half), BF),
+            vm((rows, wide), BF), vm((rows, wide), BF),
+            vm((2, rows, wide), BF), vm((2, rows, wide), BF),
             vm((2, rows, half), BF), vm((2, rows, half), BF),
             vm((slots, rows, width), BF), vm((slots, rows, gd_cols), BF),
             vm((rows, half), BF), vm((rows, half), BF), vm((rows, half), BF), vm((rows, half), BF),

time: 23.9 us -> 23 us (0.962)
  Pallas kernels: 23 us -> 22.2 us
    pallas_call x1, Pallas kernels: 22.1 us -> 21.2 us  [per_device(): pl.pallas_call(functools.partial(kernel, (n_dp, n_ex, cap, capacity, part...]
where the time goes in v3:
time: 23 us; the launch traced here: 22.8 us
  Pallas kernels  22.2 us (97%)
  between operations  0.64 us (3%)
    pallas_call x1, Pallas kernels, per_device(): pl.pallas_call(functools.partial(kernel, (n_dp, n_ex, cap, capacity, part...  21.2 us
    pallas_call x1, Pallas kernels, per_device(): pl.pallas_call(write_kernel, out_shape=tuple((jax.ShapeDtypeStruct(a.shap...  0.95 us

profile of v3, /device:TPU:0, one launch (start us, length us, event | category | flops | bytes accessed | tf_op | source)
XLA Modules:
  0.0 22.8 jit_solution(6195082617883345959)
XLA Ops:
  0.6 21.2 %shard_map.94 = (bf16[128,1024]{1,0:T(8,128)(2,1)S(1)}, bf16[128,1024]{1,0:T(8,128)(2,1)S(1)}, bf16[384,512]{1,0:T(8,128)(2,1)S(1)}) custom-call(s32[8,128]{1,0:T(8,128)} %bitcast.3, f32[8,128]{1,0:T(8,128)} %bitcast.4, bf16[128,1024]{1,0:T(8,128)(2,1)} %tok_hbm.1, bf16[128,1024]{1,0:T(8,128)(2,1)} %cot_hbm.1, bf16[1,2048,384]{2,1,0:T(8,128)(2,1)} %wg_hbm.1, ...), custom_call_target="tpu_custom_call" | custom-call | tf_op jit(solution)/shard_map/pallas_call | solution.py:332
  21.9 0.9 %shard_map.95 = (bf16[128,1024]{1,0:T(8,128)(2,1)}, bf16[128,1024]{1,0:T(8,128)(2,1)}, bf16[384,512]{1,0:T(8,128)(2,1)}) custom-call(bf16[128,1024]{1,0:T(8,128)(2,1)S(1)} %get-tuple-element.9.a, bf16[128,1024]{1,0:T(8,128)(2,1)S(1)} %get-tuple-element.10.b, bf16[384,512]{1,0:T(8,128)(2,1)S(1)} %get-tuple-element.11.c), custom_call_target="tpu_custom_call" | custom-call | tf_op jit(solution)/shard_map/pallas_call | solution.py:358

commit v4 on v3

--- a/solution.py
+++ b/solution.py
@@ -201,16 +201,16 @@
     hd[d] = hidden
     hd_send = []
     gd_send = []
+
+    loads[4].wait()
+    ps_o[...] = mm(hidden, wd[:, half_ds(other)]).astype(BF)
+    ex_o = remote(ps_o, pr_o, ex_ss.at[0], ex_rs.at[0], partner)
+    ex_o.start()
     if fused:
         for k in range(1, n_dp):
             c = remote(hd.at[d], hd.at[d], hd_ss.at[k - 1], hd_rs.at[k - 1], dp_peer(k))
             c.start()
             hd_send.append(c)
-
-    loads[4].wait()
-    ps_o[...] = mm(hidden, wd[:, half_ds(other)]).astype(BF)
-    ex_o = remote(ps_o, pr_o, ex_ss.at[0], ex_rs.at[0], partner)
-    ex_o.start()
     for k in range(1, n_ex):
         g_send[k - 1].wait_recv()
         g_fwd[k].start()
@@ -236,6 +236,15 @@
     for c in g_fwd:
         c.wait_recv()
     unpack(gp, gr, other)
+    hgrad = hgrad + mm_nt(gr[other], wd[:, half_ds(other)])
+    gate_term = (hgrad * up * sig * (1.0 + gate * (1.0 - sig))).astype(BF)
+    up_term = (hgrad * act).astype(BF)
+
+    ps_g[...] = (
+        mm_nt(gate_term, wg[half_ds(other), :]) + mm_nt(up_term, wu[half_ds(other), :])
+    ).astype(BF)
+    ex_g = remote(ps_g, pr_g, ex_ss.at[1], ex_rs.at[1], partner)
+    ex_g.start()
     if fused:
         for k in range(1, n_dp):
             at = lax.rem(d + k, n_dp) * blk
@@ -248,15 +257,6 @@
             )
             c.start()
             gd_send.append(c)
-    hgrad = hgrad + mm_nt(gr[other], wd[:, half_ds(other)])
-    gate_term = (hgrad * up * sig * (1.0 + gate * (1.0 - sig))).astype(BF)
-    up_term = (hgrad * act).astype(BF)
-
-    ps_g[...] = (
-        mm_nt(gate_term, wg[half_ds(other), :]) + mm_nt(up_term, wu[half_ds(other), :])
-    ).astype(BF)
-    ex_g = remote(ps_g, pr_g, ex_ss.at[1], ex_rs.at[1], partner)
-    ex_g.start()
     own_g = (
         (mm_nt(gate_term, wg[half_ds(t), :]) + mm_nt(up_term, wu[half_ds(t), :])).astype(BF).astype(F32)
     )

time: 23 us -> 22.9 us (level)
  no operation moved by 1% of the time
where the time goes in v4:
time: 22.9 us; the launch traced here: 22.7 us
  Pallas kernels  22.1 us (97%)
  between operations  0.64 us (3%)
    pallas_call x1, Pallas kernels, per_device(): pl.pallas_call(functools.partial(kernel, (n_dp, n_ex, cap, capacity, part...  21.1 us
    pallas_call x1, Pallas kernels, per_device(): pl.pallas_call(write_kernel, out_shape=tuple((jax.ShapeDtypeStruct(a.shap...  0.95 us

profile of v4, /device:TPU:0, one launch (start us, length us, event | category | flops | bytes accessed | tf_op | source)
XLA Modules:
  0.0 22.7 jit_solution(10421217483396260101)
XLA Ops:
  0.6 21.1 %shard_map.94 = (bf16[128,1024]{1,0:T(8,128)(2,1)S(1)}, bf16[128,1024]{1,0:T(8,128)(2,1)S(1)}, bf16[384,512]{1,0:T(8,128)(2,1)S(1)}) custom-call(s32[8,128]{1,0:T(8,128)} %bitcast.3, f32[8,128]{1,0:T(8,128)} %bitcast.4, bf16[128,1024]{1,0:T(8,128)(2,1)} %tok_hbm.1, bf16[128,1024]{1,0:T(8,128)(2,1)} %cot_hbm.1, bf16[1,2048,384]{2,1,0:T(8,128)(2,1)} %wg_hbm.1, ...), custom_call_target="tpu_custom_call" | custom-call | tf_op jit(solution)/shard_map/pallas_call | solution.py:332
  21.8 0.9 %shard_map.95 = (bf16[128,1024]{1,0:T(8,128)(2,1)}, bf16[128,1024]{1,0:T(8,128)(2,1)}, bf16[384,512]{1,0:T(8,128)(2,1)}) custom-call(bf16[128,1024]{1,0:T(8,128)(2,1)S(1)} %get-tuple-element.9.a, bf16[128,1024]{1,0:T(8,128)(2,1)S(1)} %get-tuple-element.10.b, bf16[384,512]{1,0:T(8,128)(2,1)S(1)} %get-tuple-element.11.c), custom_call_target="tpu_custom_call" | custom-call | tf_op jit(solution)/shard_map/pallas_call | solution.py:358
